TPU v7x, 32 devices: a whole 2x2x4 slice. The times are simulated.
32 devices in a mesh: videos: 2 (over y), ha: 4 (over z), wa: 2 (over x), ta: 2 (over core).
Axes of the slice: x: 2, y: 2, z: 4, core: 2. Of those that a mesh axis runs over, the one named last changes fastest.
Arguments:
- latents: bfloat16 [12, 8, 64, 512], P(('videos', 'ta'), 'ha', 'wa'), parts along dimension 0, may hold values from -200 to 200
- norm1_gain: float32 [512], replicated, may hold values from 0.25 to 1.75
- norm1_shift: float32 [512], replicated, may hold values from -2.5 to 2.5
- up_weight: bfloat16 [3, 3, 512, 256], replicated, may hold values from -0.1875 to 0.1875
- norm2_gain: float32 [256], replicated, may hold values from 0.25 to 1.75
- norm2_shift: float32 [256], replicated, may hold values from -2.5 to 2.5
- conv_a: bfloat16 [3, 3, 3, 256, 256], replicated, may hold values from -0.078125 to 0.078125
- norm3_gain: float32 [256], replicated, may hold values from 0.25 to 1.75
- norm3_shift: float32 [256], replicated, may hold values from -2.5 to 2.5
- conv_b: bfloat16 [3, 3, 3, 256, 256], replicated, may hold values from -0.078125 to 0.078125
Outputs:
- decoded: bfloat16 [12, 16, 128, 256], P(('videos', 'ta'), 'ha', 'wa'), parts along dimension 0
There are 2 independent parts, one for each index of `videos`. A program takes and returns all parts, laid end to end along the dimension named above; an argument that names none is the same for every part. Nothing has to cross between parts.
All inputs are finite; a program needn't handle non-finite values.
Results may differ from a plain program's by a relative error of at most 0.008.
Values may be sent and summed in bfloat16 or wider, within the bound.
A program may use at most 64 MiB of HBM per device.

v0:
```python
import jax
import jax.numpy as jnp
from jax import lax
from jax.sharding import PartitionSpec as P

GROUPS = 32


EPSILON = 1e-06


def passed_along(block, axis, distance):
    devices = range(lax.axis_size(axis))
    route = [(i - distance, i) for i in devices if i - distance in devices]
    return lax.ppermute(block, axis, route)


def padded_2(x, sides, width):
    for axis, dim in sides:
        size, length = (lax.axis_size(axis), x.shape[dim])
        up = [(i, (i + 1) % size) for i in range(size - 1)]
        down = [(j, i) for i, j in up]
        last = lax.slice_in_dim(x, length - width, length, axis=dim)
        initial = lax.slice_in_dim(x, 0, width, axis=dim)
        before = lax.ppermute(last, axis, up)
        after = lax.ppermute(initial, axis, down)
        x = jnp.concatenate([before, x, after], axis=dim)
    return x


def activate(values, sample, scale_vec, shift_vec):
    channels = values.shape[-1]
    group_width = channels // GROUPS
    grouped = sample.reshape(-1, GROUPS, group_width)
    entries = (
        grouped.shape[0]
        * group_width
        * lax.axis_size("ha")
        * lax.axis_size("wa")
        * lax.axis_size("ta")
    )
    totals, squares = lax.psum(
        (jnp.sum(grouped, axis=(0, 2)), jnp.sum(grouped * grouped, axis=(0, 2))), ("ha", "wa", "ta")
    )
    average = totals / entries
    spread = squares / entries - average * average
    scaling = lax.rsqrt(spread + EPSILON)
    normed = (values - jnp.repeat(average, group_width)) * jnp.repeat(
        scaling, group_width
    ) * scale_vec + shift_vec
    return jax.nn.silu(normed).astype(jnp.bfloat16)


def parity_merge(lead_part, mid_part, tail_part, axis_pos):
    pad_end = [(0, 0)] * lead_part.ndim
    pad_front = [(0, 0)] * lead_part.ndim
    pad_end[axis_pos] = (0, 1)
    pad_front[axis_pos] = (1, 0)
    even_part = jnp.pad(lead_part, pad_end) + jnp.pad(tail_part, pad_front)
    odd_part = jnp.pad(mid_part, pad_end)
    stacked = jnp.stack([even_part, odd_part], axis=axis_pos + 1)
    new_shape = list(even_part.shape)
    new_shape[axis_pos] = new_shape[axis_pos] * 2
    return stacked.reshape(new_shape)


def spread_taps(source, kernel):
    frames, height, across, channels = source.shape
    flattened = source.reshape(-1, channels)
    products = [
        [
            jnp.dot(flattened, kernel[tap_y, tap_x], preferred_element_type=jnp.float32).reshape(
                frames, height, across, -1
            )
            for tap_x in range(3)
        ]
        for tap_y in range(3)
    ]
    columns = [
        parity_merge(products[0][tap_x], products[1][tap_x], products[2][tap_x], 1)
        for tap_x in range(3)
    ]
    return parity_merge(columns[0], columns[1], columns[2], 2)


def valid_conv(padded, kernel, frames, height, across):
    result = jnp.zeros((frames * height * across, kernel.shape[-1]), jnp.float32)
    for step_t in range(3):
        for step_y in range(3):
            for step_x in range(3):
                window = padded[
                    step_t : step_t + frames, step_y : step_y + height, step_x : step_x + across
                ]
                result = result + jnp.dot(
                    window.reshape(-1, window.shape[-1]),
                    kernel[step_t, step_y, step_x],
                    preferred_element_type=jnp.float32,
                )
    return result.reshape(frames, height, across, -1)


def causal_extend(values):
    earlier = passed_along(values[-2:], "ta", 1)
    opening = jnp.concatenate([values[:1], values[:1]], axis=0)
    earlier = jnp.where(lax.axis_index("ta") == 0, opening, earlier)
    return jnp.concatenate([earlier, values], axis=0)


def bordered_one(values):
    return padded_2(values, (("ha", 1), ("wa", 2)), 1)


def per_device(
    latents,
    norm1_gain,
    norm1_shift,
    up_weight,
    norm2_gain,
    norm2_shift,
    conv_a,
    norm3_gain,
    norm3_shift,
    conv_b,
):
    frames, height, across, channels = latents.shape
    latent_f = latents.astype(jnp.float32)
    activated = activate(latent_f, latent_f, norm1_gain, norm1_shift)
    spilled = spread_taps(activated, up_weight)
    from_below = passed_along(spilled[:, 0], "ha", -1)
    row_fixed = spilled[:, 1 : 2 * height + 1]
    row_fixed = jnp.concatenate(
        [row_fixed[:, :-1], row_fixed[:, -1:] + from_below[:, None]], axis=1
    )
    beside = passed_along(row_fixed[:, :, 0], "wa", -1)
    lifted = jnp.concatenate(
        [
            row_fixed[:, :, 1 : 2 * across],
            row_fixed[:, :, 2 * across : 2 * across + 1] + beside[:, :, None],
        ],
        axis=2,
    )
    lifted = lifted.astype(jnp.bfloat16)
    lifted_f = lifted.astype(jnp.float32)
    first_act = activate(lifted_f, lifted_f, norm2_gain, norm2_shift)
    out_h = 2 * height
    out_w = 2 * across
    hidden = valid_conv(
        bordered_one(causal_extend(first_act)), conv_a, frames, out_h, out_w
    ).astype(jnp.bfloat16)
    hidden_f = hidden.astype(jnp.float32)
    second_act = activate(hidden_f, hidden_f, norm3_gain, norm3_shift)
    framed = bordered_one(causal_extend(second_act))
    branch = valid_conv(framed, conv_b, frames, out_h, out_w)
    return (lifted_f + branch).astype(jnp.bfloat16)


def solution(mesh):
    return jax.shard_map(
        per_device,
        mesh=mesh,
        in_specs=(
            P(("videos", "ta"), "ha", "wa", None),
            P(),
            P(),
            P(),
            P(),
            P(),
            P(),
            P(),
            P(),
            P(),
        ),
        out_specs=P(("videos", "ta"), "ha", "wa", None),
        check_vma=False,
    )
```

profile of v0, /device:TPU:0, one launch (start us, length us, event | category | flops | bytes accessed | tf_op | source)
XLA Modules:
  0.0 204.1 jit_solution(1638593344820532898)
XLA Ops:
  1.4 34.9 %all-reduce.14 = (f32[32]{0:T(128)S(1)}, f32[32]{0:T(128)S(1)}) all-reduce(f32[32]{0:T(128)S(1)} %reduce_sum.77, f32[32]{0:T(128)S(1)} %reduce_sum.74), channel_id=1, replica_groups=mesh['videos'=2,'ha'=4,'wa'=2,'ta'=2] {'ha','wa','ta'}, use_global_device_ids=true, to_apply=%region_5.6 | all-reduce | flops 64 | bytes 512 | tf_op jit(solution)/shard_map/psum | solution.py:42
  50.9 1.3 collective-permute-start
  52.6 6.2 %collective-permute-done = f32[3,66,256]{2,1,0:T(8,128)S(1)} collective-permute-done((f32[3,66,256]{2,1,0:T(8,128)S(1)}, f32[3,66,256]{2,1,0:T(8,128)S(1)}, u32[]{:S(2)}, u32[]{:S(2)}) %collective-permute-start) | collective-permute-done | bytes 202784 | tf_op jit(solution)/shard_map/ppermute | solution.py:15
  59.0 1.3 collective-permute-start.1
  60.7 3.9 %collective-permute-done.1 = f32[3,4,256]{2,1,0:T(4,128)S(1)} collective-permute-done((f32[3,4,256]{2,1,0:T(4,128)S(1)}, f32[3,4,256]{2,1,0:T(4,128)S(1)}, u32[]{:S(2)}, u32[]{:S(2)}) %collective-permute-start.1) | collective-permute-done | bytes 12320 | tf_op jit(solution)/shard_map/ppermute | solution.py:15
  65.5 29.5 %all-reduce.13 = (f32[32]{0:T(128)S(1)}, f32[32]{0:T(128)S(1)}) all-reduce(f32[32]{0:T(128)S(1)} %reduce_sum.89, f32[32]{0:T(128)S(1)} %reduce_sum.83), channel_id=1, replica_groups=mesh['videos'=2,'ha'=4,'wa'=2,'ta'=2] {'ha','wa','ta'}, use_global_device_ids=true, to_apply=%region_11.12 | all-reduce | flops 64 | bytes 512 | tf_op jit(solution)/shard_map/psum | solution.py:42
  96.0 1.8 collective-permute-start.2
  100.0 1.3 collective-permute-start.4
  101.3 4.6 %collective-permute-start.3 = (bf16[5,1,64,256]{3,1,2,0:T(2,128)(2,1)S(1)}, bf16[5,1,64,256]{3,1,2,0:T(2,128)(2,1)S(1)}, u32[]{:S(2)}, u32[]{:S(2)}) collective-permute-start(bf16[5,1,64,256]{3,1,2,0:T(2,128)(2,1)S(1)} %get-tuple-element.81), channel_id=1, source_target_pairs={{0,4},{4,8},{8,12},{1,5},{5,9},{9,13},{2,6},{6,10},{10,14},{3,7},{... | collective-permute-start | bytes 491528 | tf_op jit(solution)/shard_map/ppermute | solution.py:25
  105.9 5.9 %collective-permute-done.4 = bf16[5,1,64,256]{3,1,2,0:T(2,128)(2,1)S(1)} collective-permute-done((bf16[5,1,64,256]{3,1,2,0:T(2,128)(2,1)S(1)}, bf16[5,1,64,256]{3,1,2,0:T(2,128)(2,1)S(1)}, u32[]{:S(2)}, u32[]{:S(2)}) %collective-permute-start.4) | collective-permute-done | bytes 163872 | tf_op jit(solution)/shard_map/ppermute | solution.py:26
  114.4 1.5 collective-permute-start.6
  117.2 1.7 pad_maximum_fusion.15
  120.1 2.3 %maximum_maximum_fusion = (bf16[5,6,65,256]{3,1,2,0:T(8,128)(2,1)S(1)}, bf16[5,6,65,256]{3,1,2,0:T(8,128)(2,1)S(1)}) fusion(bf16[5,1,64,256]{3,1,2,0:T(2,128)(2,1)S(1)} %collective-permute-done.4, bf16[3,4,64,256]{3,1,2,0:T(4,128)(2,1)S(1)} %fusion.13, bf16[2,4,64,256]{3,1,2,0:T(4,128)(2,1)S(1)} %maximum_select_fusion, ...), kind=kLoop, calls=%fused_computation.5 | loop fusion | flops 9984000 | bytes 3010560 | tf_op jit(solution)/shard_map/concatenate | solution.py:27
  122.4 1.6 fusion.182
  124.0 1.3 fusion.183
  133.7 30.7 %all-reduce.12 = (f32[32]{0:T(128)S(1)}, f32[32]{0:T(128)S(1)}) all-reduce(f32[32]{0:T(128)S(1)} %reduce_sum.113, f32[32]{0:T(128)S(1)} %reduce_sum.110), channel_id=1, replica_groups=mesh['videos'=2,'ha'=4,'wa'=2,'ta'=2] {'ha','wa','ta'}, use_global_device_ids=true, to_apply=%region_17.18 | all-reduce | flops 64 | bytes 512 | tf_op jit(solution)/shard_map/psum | solution.py:42
  165.6 1.8 collective-permute-start.7
  169.4 1.3 collective-permute-start.9
  170.7 4.6 %collective-permute-start.8 = (bf16[5,1,64,256]{3,1,2,0:T(2,128)(2,1)S(1)}, bf16[5,1,64,256]{3,1,2,0:T(2,128)(2,1)S(1)}, u32[]{:S(2)}, u32[]{:S(2)}) collective-permute-start(bf16[5,1,64,256]{3,1,2,0:T(2,128)(2,1)S(1)} %get-tuple-element.77), channel_id=1, source_target_pairs={{0,4},{4,8},{8,12},{1,5},{5,9},{9,13},{2,6},{6,10},{10,14},{3,7},{... | collective-permute-start | bytes 491528 | tf_op jit(solution)/shard_map/ppermute | solution.py:25
  175.3 6.0 %collective-permute-done.9 = bf16[5,1,64,256]{3,1,2,0:T(2,128)(2,1)S(1)} collective-permute-done((bf16[5,1,64,256]{3,1,2,0:T(2,128)(2,1)S(1)}, bf16[5,1,64,256]{3,1,2,0:T(2,128)(2,1)S(1)}, u32[]{:S(2)}, u32[]{:S(2)}) %collective-permute-start.9) | collective-permute-done | bytes 163872 | tf_op jit(solution)/shard_map/ppermute | solution.py:26
  183.8 1.3 collective-permute-start.11
  186.4 1.7 pad_maximum_fusion.6
  189.5 2.3 %maximum_maximum_fusion.1 = (bf16[5,6,65,256]{3,1,2,0:T(8,128)(2,1)S(1)}, bf16[5,6,65,256]{3,1,2,0:T(8,128)(2,1)S(1)}) fusion(bf16[5,1,64,256]{3,1,2,0:T(2,128)(2,1)S(1)} %collective-permute-done.9, bf16[3,4,64,256]{3,1,2,0:T(4,128)(2,1)S(1)} %fusion.14, bf16[2,4,64,256]{3,1,2,0:T(4,128)(2,1)S(1)} %maximum_select_fusion.1, ...), kind=kLoop, calls=%fused_computation.7 | loop fusion | flops 9984000 | bytes 3010560 | tf_op jit(solution)/shard_map/concatenate | solution.py:27
  191.8 1.6 fusion.180
  (205 shorter events, 52.3 us)
Async XLA Ops:
  50.9 44.4 %copy-start.2 = (f32[256]{0:T(256)S(1)}, f32[256]{0:T(256)}, u32[]{:S(2)}) copy-start(f32[256]{0:T(256)} %param.15) | copy-start | bytes 3076
  50.9 44.4 %copy-start.3 = (f32[256]{0:T(256)S(1)}, f32[256]{0:T(256)}, u32[]{:S(2)}) copy-start(f32[256]{0:T(256)} %param.14) | copy-start | bytes 3076
  50.9 7.8 %collective-permute-start = (f32[3,66,256]{2,1,0:T(8,128)S(1)}, f32[3,66,256]{2,1,0:T(8,128)S(1)}, u32[]{:S(2)}, u32[]{:S(2)}) collective-permute-start(f32[3,66,256]{2,1,0:T(8,128)S(1)} %get-tuple-element.53), channel_id=1, source_target_pairs={{4,0},{8,4},{12,8},{5,1},{9,5},{13,9},{6,2},{10,6},{14,10},{7,3},{... | collective-permute-start | bytes 608264 | tf_op jit(solution)/shard_map/ppermute | solution.py:15
  59.0 5.6 %collective-permute-start.1 = (f32[3,4,256]{2,1,0:T(4,128)S(1)}, f32[3,4,256]{2,1,0:T(4,128)S(1)}, u32[]{:S(2)}, u32[]{:S(2)}) collective-permute-start(f32[3,4,256]{2,1,0:T(4,128)S(1)} %fusion.176), channel_id=1, source_target_pairs={{2,0},{3,1},{6,4},{7,5},{10,8},{11,9},{14,12},{15,13},{18,16},{19,... | collective-permute-start | bytes 36872 | tf_op jit(solution)/shard_map/ppermute | solution.py:15
  96.0 2.9 %collective-permute-start.2 = (bf16[2,4,64,256]{3,1,2,0:T(4,128)(2,1)S(1)}, bf16[2,4,64,256]{3,1,2,0:T(4,128)(2,1)S(1)}, u32[]{:S(2)}, u32[]{:S(2)}) collective-permute-start(bf16[2,4,64,256]{3,1,2,0:T(4,128)(2,1)S(1)} %slice.594), channel_id=1, source_target_pairs={{0,1},{2,3},{4,5},{6,7},{8,9},{10,11},{12,13},{14,15},{16,17},{18,... | collective-permute-start | bytes 786440 | tf_op jit(solution)/shard_map/ppermute | solution.py:15
  97.9 19.0 %copy-start = (bf16[3,3,3,256,256]{4,3,2,1,0:T(8,128)(2,1)S(1)}, bf16[3,3,3,256,256]{4,3,2,1,0:T(8,128)(2,1)}, u32[]{:S(2)}) copy-start(bf16[3,3,3,256,256]{4,3,2,1,0:T(8,128)(2,1)} %param.16) | copy-start | bytes 10616836
  100.0 11.9 %collective-permute-start.4 = (bf16[5,1,64,256]{3,1,2,0:T(2,128)(2,1)S(1)}, bf16[5,1,64,256]{3,1,2,0:T(2,128)(2,1)S(1)}, u32[]{:S(2)}, u32[]{:S(2)}) collective-permute-start(bf16[5,1,64,256]{3,1,2,0:T(2,128)(2,1)S(1)} %get-tuple-element.82), channel_id=1, source_target_pairs={{4,0},{8,4},{12,8},{5,1},{9,5},{13,9},{6,2},{10,6},{14,10},{7,3},{... | collective-permute-start | bytes 491528 | tf_op jit(solution)/shard_map/ppermute | solution.py:26
  101.3 11.8 %collective-permute-start.3 = (bf16[5,1,64,256]{3,1,2,0:T(2,128)(2,1)S(1)}, bf16[5,1,64,256]{3,1,2,0:T(2,128)(2,1)S(1)}, u32[]{:S(2)}, u32[]{:S(2)}) collective-permute-start(bf16[5,1,64,256]{3,1,2,0:T(2,128)(2,1)S(1)} %get-tuple-element.81), channel_id=1, source_target_pairs={{0,4},{4,8},{8,12},{1,5},{5,9},{9,13},{2,6},{6,10},{10,14},{3,7},{... | collective-permute-start | bytes 491528 | tf_op jit(solution)/shard_map/ppermute | solution.py:25
  113.1 6.2 %collective-permute-start.5 = (bf16[5,6,1,256]{3,1,2,0:T(8,128)(2,1)S(1)}, bf16[5,6,1,256]{3,1,2,0:T(8,128)(2,1)S(1)}, u32[]{:S(2)}, u32[]{:S(2)}) collective-permute-start(bf16[5,6,1,256]{3,1,2,0:T(8,128)(2,1)S(1)} %get-tuple-element.61), channel_id=1, source_target_pairs={{0,2},{1,3},{4,6},{5,7},{8,10},{9,11},{12,14},{13,15},{16,18},{17,... | collective-permute-start | bytes 46088 | tf_op jit(solution)/shard_map/ppermute | solution.py:25
  114.4 5.7 %collective-permute-start.6 = (bf16[5,6,1,256]{3,1,2,0:T(8,128)(2,1)S(1)}, bf16[5,6,1,256]{3,1,2,0:T(8,128)(2,1)S(1)}, u32[]{:S(2)}, u32[]{:S(2)}) collective-permute-start(bf16[5,6,1,256]{3,1,2,0:T(8,128)(2,1)S(1)} %get-tuple-element.62), channel_id=1, source_target_pairs={{2,0},{3,1},{6,4},{7,5},{10,8},{11,9},{14,12},{15,13},{18,16},{19,... | collective-permute-start | bytes 46088 | tf_op jit(solution)/shard_map/ppermute | solution.py:26
  132.4 32.4 %copy-start.4 = (f32[256]{0:T(256)S(1)}, f32[256]{0:T(256)}, u32[]{:S(2)}) copy-start(f32[256]{0:T(256)} %param.18) | copy-start | bytes 3076
  132.4 32.4 %copy-start.5 = (f32[256]{0:T(256)S(1)}, f32[256]{0:T(256)}, u32[]{:S(2)}) copy-start(f32[256]{0:T(256)} %param.17) | copy-start | bytes 3076
  165.5 20.6 %copy-start.1 = (bf16[3,3,3,256,256]{4,3,2,1,0:T(8,128)(2,1)S(1)}, bf16[3,3,3,256,256]{4,3,2,1,0:T(8,128)(2,1)}, u32[]{:S(2)}) copy-start(bf16[3,3,3,256,256]{4,3,2,1,0:T(8,128)(2,1)} %param.19) | copy-start | bytes 10616836
  165.6 2.7 %collective-permute-start.7 = (bf16[2,4,64,256]{3,1,2,0:T(4,128)(2,1)S(1)}, bf16[2,4,64,256]{3,1,2,0:T(4,128)(2,1)S(1)}, u32[]{:S(2)}, u32[]{:S(2)}) collective-permute-start(bf16[2,4,64,256]{3,1,2,0:T(4,128)(2,1)S(1)} %slice.620), channel_id=1, source_target_pairs={{0,1},{2,3},{4,5},{6,7},{8,9},{10,11},{12,13},{14,15},{16,17},{18,... | collective-permute-start | bytes 786440 | tf_op jit(solution)/shard_map/ppermute | solution.py:15
  169.4 11.9 %collective-permute-start.9 = (bf16[5,1,64,256]{3,1,2,0:T(2,128)(2,1)S(1)}, bf16[5,1,64,256]{3,1,2,0:T(2,128)(2,1)S(1)}, u32[]{:S(2)}, u32[]{:S(2)}) collective-permute-start(bf16[5,1,64,256]{3,1,2,0:T(2,128)(2,1)S(1)} %get-tuple-element.78), channel_id=1, source_target_pairs={{4,0},{8,4},{12,8},{5,1},{9,5},{13,9},{6,2},{10,6},{14,10},{7,3},{... | collective-permute-start | bytes 491528 | tf_op jit(solution)/shard_map/ppermute | solution.py:26
  170.7 11.8 %collective-permute-start.8 = (bf16[5,1,64,256]{3,1,2,0:T(2,128)(2,1)S(1)}, bf16[5,1,64,256]{3,1,2,0:T(2,128)(2,1)S(1)}, u32[]{:S(2)}, u32[]{:S(2)}) collective-permute-start(bf16[5,1,64,256]{3,1,2,0:T(2,128)(2,1)S(1)} %get-tuple-element.77), channel_id=1, source_target_pairs={{0,4},{4,8},{8,12},{1,5},{5,9},{9,13},{2,6},{6,10},{10,14},{3,7},{... | collective-permute-start | bytes 491528 | tf_op jit(solution)/shard_map/ppermute | solution.py:25
  182.5 6.0 %collective-permute-start.10 = (bf16[5,6,1,256]{3,1,2,0:T(8,128)(2,1)S(1)}, bf16[5,6,1,256]{3,1,2,0:T(8,128)(2,1)S(1)}, u32[]{:S(2)}, u32[]{:S(2)}) collective-permute-start(bf16[5,6,1,256]{3,1,2,0:T(8,128)(2,1)S(1)} %get-tuple-element.57), channel_id=1, source_target_pairs={{0,2},{1,3},{4,6},{5,7},{8,10},{9,11},{12,14},{13,15},{16,18},{17,... | collective-permute-start | bytes 46088 | tf_op jit(solution)/shard_map/ppermute | solution.py:25
  183.8 5.7 %collective-permute-start.11 = (bf16[5,6,1,256]{3,1,2,0:T(8,128)(2,1)S(1)}, bf16[5,6,1,256]{3,1,2,0:T(8,128)(2,1)S(1)}, u32[]{:S(2)}, u32[]{:S(2)}) collective-permute-start(bf16[5,6,1,256]{3,1,2,0:T(8,128)(2,1)S(1)} %get-tuple-element.58), channel_id=1, source_target_pairs={{2,0},{3,1},{6,4},{7,5},{10,8},{11,9},{14,12},{15,13},{18,16},{19,... | collective-permute-start | bytes 46088 | tf_op jit(solution)/shard_map/ppermute | solution.py:26
where the time goes:
time: 205 us; the launch traced here: 204 us
  blocking collectives  95.1 us (46%)
  waiting for transfers between devices  28 us (14%)
  matrix products  24.9 us (12%)
  starting transfers between devices  23.2 us (11%)
  other arithmetic  18.4 us (9%)
  local copies, waits for them, and re-layouts  13 us (6%)
    psum x3, blocking collectives, activate(): lax.psum((jnp.sum(grouped, axis=(0, 2)), jnp.sum(grouped * grouped, axis=...  95.1 us
    dot_general x54, matrix products, valid_conv(): jnp.dot(window.reshape(-1, window.shape[-1]), kernel[step_t, step_y, step...  14.4 us
    ppermute x4, waiting for transfers between devices, padded_2(): after = lax.ppermute(initial, axis, down)  13.7 us
    ppermute x4, waiting for transfers between devices, passed_along(): return lax.ppermute(block, axis, route)  12 us
    ppermute x4, starting transfers between devices, padded_2(): before = lax.ppermute(last, axis, up)  11.7 us
    concatenate x6, other arithmetic, padded_2(): x = jnp.concatenate([before, x, after], axis=dim)  10.1 us
    slice x56, local copies, waits for them, and re-layouts, valid_conv(): padded[step_t:step_t + frames, step_y:step_y + height, step_x:step_x + ac...  8.07 us
    dot_general x6, matrix products, spread_taps(): jnp.dot(flattened, kernel[tap_y, tap_x], preferred_element_type=jnp.float32)  6.97 us
  transfers between devices with their start and end apart: 12, of which 10 were waited for; matrix products, arithmetic and copies ran while one was open for 4% of the time, Pallas kernels for 0%

commit v1 on v0

v1 whole, which is shorter than its diff:
```python
import functools
import jax
import jax.numpy as jnp
from jax import lax
from jax.experimental import pallas as pl
from jax.experimental.pallas import tpu as pltpu
from jax.sharding import PartitionSpec as P

GROUPS = 32
EPSILON = 1e-06
MESH = pl.DeviceIdType.MESH
F32 = jnp.float32
BF16 = jnp.bfloat16


def group_sum(x, width):
    pieces = []
    for k in range(x.shape[1] // 128):
        piece = x[:, k * 128 : (k + 1) * 128]
        lane = lax.broadcasted_iota(jnp.int32, piece.shape, 1)
        step = 1
        while step < width:
            ahead = pltpu.roll(piece, 128 - step, 1)
            behind = pltpu.roll(piece, step, 1)
            piece = piece + jnp.where((lane & step) == 0, ahead, behind)
            step *= 2
        pieces.append(piece)
    return jnp.concatenate(pieces, axis=1)


def half_silu(h):
    return h + h * jnp.tanh(h)


def kernel(
    sizes,
    lat,
    g1,
    s1,
    up_hbm,
    g2,
    s2,
    ca_hbm,
    g3,
    s3,
    cb_hbm,
    out,
    up_w,
    ca_w,
    cb_w,
    lat_row,
    lat_col,
    lat_stage,
    up_in,
    raw2,
    raw3,
    col2,
    col3,
    stage2,
    stage3,
    conv_in,
    merged,
    st1,
    st2,
    st3,
    w_sem,
    halo_send,
    halo_recv,
    stat_send,
    stat_recv,
):
    n_ha, n_wa, n_ta = sizes
    n_all = n_ha * n_wa * n_ta
    ha, wa, ta = lax.axis_index("ha"), lax.axis_index("wa"), lax.axis_index("ta")
    me = (ha * n_wa + wa) * n_ta + ta
    frames, height, across, c1 = lat.shape
    c2 = up_w.shape[-1]
    out_h, out_w = 2 * height, 2 * across

    weights = [
        pltpu.make_async_copy(a, b, w_sem.at[i])
        for i, (a, b) in enumerate(((up_hbm, up_w), (ca_hbm, ca_w), (cb_hbm, cb_w)))
    ]
    for w in weights:
        w.start()

    lat_row[...] = jnp.zeros_like(lat_row)
    lat_col[...] = jnp.zeros_like(lat_col)
    for raw, col in ((raw2, col2), (raw3, col3)):
        col[...] = jnp.zeros_like(col)
        for f in range(frames + 2):
            for r in (0, out_h + 1):
                raw[f, r] = jnp.zeros(raw.shape[2:], raw.dtype)

    def peer(d):
        p = lax.rem(me + d, n_all)
        return {"ha": p // (n_wa * n_ta), "wa": (p // n_ta) % n_wa, "ta": p % n_ta}

    barrier = pltpu.get_barrier_semaphore()

    @pl.loop(1, n_all)
    def _(d):
        pl.semaphore_signal(barrier, inc=1, device_id=peer(d), device_id_type=MESH)

    def set_stats(st, x):
        rows = x.shape[0]
        mean = jnp.sum(x, axis=0, keepdims=True) * (1.0 / rows)
        centred = x - mean
        st[0, 0:1, :] = mean
        st[0, 1:2, :] = jnp.sum(centred * centred, axis=0, keepdims=True)

    def send_stats(st, i):
        @pl.loop(1, n_all)
        def _(d):
            pltpu.make_async_remote_copy(
                src_ref=st.at[0],
                dst_ref=st.at[d],
                send_sem=stat_send.at[i],
                recv_sem=stat_recv.at[i],
                device_id=peer(d),
                device_id_type=MESH,
            ).start()

    def all_stats(st, i, sem):
        pltpu.make_async_copy(st.at[1:n_all], st.at[1:n_all], sem.at[i]).wait()

    def affine(st, i, rows, gain, shift):
        all_stats(st, i, stat_recv)
        c = st.shape[-1]
        width = c // GROUPS
        v = st[...]
        mean_c = jnp.broadcast_to(jnp.sum(v, axis=0)[0:1] * (1.0 / n_all), (8, c))
        mean = group_sum(mean_c, width) * (1.0 / width)
        kind = lax.broadcasted_iota(jnp.int32, v.shape, 1)
        off = v - mean[0:2][None]
        parts = jnp.sum(jnp.where(kind == 0, off * off * float(rows), v), axis=0)
        both = jnp.broadcast_to(parts[0:1] + parts[1:2], (8, c))
        spread = group_sum(both, width) * (1.0 / (width * rows * n_all))
        scaling = lax.rsqrt(spread + EPSILON)
        factor = 0.5 * scaling[0:1] * gain[...]
        return mean[0:1], factor, 0.5 * shift[...]

    def inside(dta, dha, dwa):
        h, w, t = ha + dha, wa + dwa, ta + dta
        ok = (h >= 0) & (h < n_ha) & (w >= 0) & (w < n_wa)
        return ok & (t >= 0) & (t < n_ta)

    def neighbour(dta, dha, dwa):
        return {"ha": ha + dha, "wa": wa + dwa, "ta": ta + dta}

    def remote(src, dst, i, move):
        dta, dha, dwa = move
        k = dta * 9 + (dha + 1) * 3 + dwa + 1
        return pltpu.make_async_remote_copy(
            src_ref=src,
            dst_ref=dst,
            send_sem=halo_send.at[i, k],
            recv_sem=halo_recv.at[i, k],
            device_id=neighbour(*move),
            device_id_type=MESH,
        )

    def start(copies):
        for move, copy in copies:
            pl.when(inside(*move))(copy.start)

    def sent(copies):
        for move, copy in copies:
            pl.when(inside(*move))(copy.wait_send)

    def received(copies):
        for move, copy in copies:
            dta, dha, dwa = move
            pl.when(inside(-dta, -dha, -dwa))(copy.wait_recv)

    def field_copies(i, raw, col, stage, dta):
        copies = []
        f_from, f_to, count = (0, 2, frames) if dta == 0 else (frames - 2, 0, 2)
        for dha in (-1, 0, 1):
            r_from, r_to, n_r = {-1: (0, out_h + 1, 1), 0: (0, 1, out_h), 1: (out_h - 1, 0, 1)}[dha]
            for dwa in (0, -1, 1):
                move = (dta, dha, dwa)
                if move == (0, 0, 0):
                    continue
                fd, rd = pl.ds(f_to, count), pl.ds(r_to, n_r)
                if dwa == 0:
                    src = raw.at[pl.ds(f_from + 2, count), pl.ds(r_from + 1, n_r)]
                    dst = raw.at[fd, rd]
                else:
                    side = (dwa + 1) // 2
                    src = stage.at[side, pl.ds(f_from, count), pl.ds(r_from, n_r)]
                    dst = col.at[1 - side, fd, rd]
                copies.append((move, remote(src, dst, i, move)))
        return copies

    set_stats(st1, lat[...].astype(F32).reshape(-1, c1))
    for f in range(frames):
        for r in range(height):
            lat_stage[f, r] = lat[f, r, 0:16, :].astype(F32)[0:1]
    pl.semaphore_wait(barrier, n_all - 1)
    send_stats(st1, 0)
    lat_copies = [
        ((0, -1, 0), remote(lat.at[:, 0], lat_row, 0, (0, -1, 0))),
        ((0, 0, -1), remote(lat_stage, lat_col.at[:, pl.ds(0, height)], 0, (0, 0, -1))),
        (
            (0, -1, -1),
            remote(
                lat_stage.at[:, pl.ds(0, 1)], lat_col.at[:, pl.ds(height, 1)], 0, (0, -1, -1)
            ),
        ),
    ]
    start(lat_copies)
    mean, factor, offset = affine(st1, 0, frames * height * across, g1, s1)
    received(lat_copies)
    row_in = lax.broadcasted_iota(jnp.int32, (across, 1), 0)
    right_ok = (wa < n_wa - 1).astype(F32)
    left_ok = (wa > 0).astype(F32)
    below_ok = (ha < n_ha - 1).astype(F32)
    above_ok = (ha > 0).astype(F32)

    def up_row(f, r, x, keep):
        y = half_silu((x - mean) * factor + offset) * keep
        edge = half_silu((lat_col[f, r] - mean) * factor + offset) * (keep * right_ok)
        moved = jnp.where(row_in == across - 1, edge, pltpu.roll(y, across - 1, 0))
        up_in[f, r, :, 0:c1] = y.astype(BF16)
        up_in[f, r, :, c1 : 2 * c1] = moved.astype(BF16)

    @pl.loop(0, frames)
    def _(f):
        for r in range(height):
            up_row(f, r, lat[f, r].astype(F32), 1.0)
        up_row(f, height, lat_row[f].astype(F32), below_ok)

    weights[0].wait()

    def tap(dy, dx, ky, kx):
        a = up_in[:, dy : dy + height, :, dx * c1 : (dx + 1) * c1].reshape(-1, c1)
        return jnp.dot(a, up_w[ky, kx], preferred_element_type=F32)

    lifted = {
        (0, 0): lambda: tap(0, 0, 1, 1),
        (0, 1): lambda: tap(0, 0, 1, 2) + tap(0, 1, 1, 0),
        (1, 0): lambda: tap(0, 0, 2, 1) + tap(1, 0, 0, 1),
        (1, 1): lambda: tap(0, 0, 2, 2) + tap(0, 1, 2, 0) + tap(1, 0, 0, 2) + tap(1, 1, 0, 0),
    }
    for (a, b), make in lifted.items():
        block = make().astype(BF16).reshape(frames, height, across, c2)
        for i in range(height):
            raw2[2 : 2 + frames, 1 + 2 * i + a, b * across : (b + 1) * across, :] = block[:, i]

    def norm_conv(i, raw, col, stage, st, gain, shift, w, w_copy):
        own = raw[2 : 2 + frames, 1 : 1 + out_h].astype(F32)
        set_stats(st, own.reshape(-1, c2))
        send_stats(st, i)
        for f in range(frames):
            for r in range(out_h):
                stage[0, f, r] = raw[2 + f, 1 + r, 0:16, :].astype(F32)[0:1]
                stage[1, f, r] = raw[2 + f, 1 + r, out_w - 16 : out_w, :].astype(F32)[15:16]
        here = field_copies(i, raw, col, stage, 0)
        later = field_copies(i, raw, col, stage, 1)
        start(later)
        start(here)
        mean, factor, offset = affine(st, i, frames * out_h * out_w, gain, shift)

        def one_row(f, r, keep):
            x = raw[f, r].astype(F32)
            y = half_silu((x - mean) * factor + offset)
            if keep is not None:
                y = y * keep
            even, odd = y[:across], y[across:]
            conv_in[f, r, :, 0:c2] = pltpu.roll(odd, 1, 0).astype(BF16)
            conv_in[f, r, :, c2 : 2 * c2] = even.astype(BF16)
            conv_in[f, r, :, 2 * c2 : 3 * c2] = odd.astype(BF16)
            conv_in[f, r, :, 3 * c2 : 4 * c2] = pltpu.roll(even, across - 1, 0).astype(BF16)

        def edges(f, r, keep):
            first = lax.broadcasted_iota(jnp.int32, (16, 1), 0)
            y = half_silu((col[0, f, r] - mean) * factor + offset) * (keep * left_ok)
            old = conv_in[f, r, 0:16, 0:c2].astype(F32)
            conv_in[f, r, 0:16, 0:c2] = jnp.where(first == 0, y, old).astype(BF16)
            y = half_silu((col[1, f, r] - mean) * factor + offset) * (keep * right_ok)
            old = conv_in[f, r, across - 16 : across, 3 * c2 : 4 * c2].astype(F32)
            conv_in[f, r, across - 16 : across, 3 * c2 : 4 * c2] = jnp.where(
                first == 15, y, old
            ).astype(BF16)

        def finish(f):
            one_row(f, 0, above_ok)
            one_row(f, out_h + 1, below_ok)
            edges(f, 0, above_ok)
            edges(f, out_h + 1, below_ok)
            for r in range(1, out_h + 1):
                edges(f, r, 1.0)

        @pl.loop(2, 2 + frames)
        def _(f):
            for r in range(1, out_h + 1):
                one_row(f, r, None)

        received(here)

        @pl.loop(2, 2 + frames)
        def _(f):
            finish(f)

        @pl.when(ta == 0)
        def _():
            conv_in[0] = conv_in[2]
            conv_in[1] = conv_in[2]

        received(later)

        @pl.when(ta > 0)
        def _():
            @pl.loop(0, 2)
            def _(f):
                for r in range(1, out_h + 1):
                    one_row(f, r, None)
                finish(f)

        w_copy.wait()
        results = []
        for b in range(2):
            total = None
            for dt in range(3):
                for dy in range(3):
                    window = conv_in[
                        dt : dt + frames, dy : dy + out_h, :, b * c2 : (b + 3) * c2
                    ].reshape(-1, 3 * c2)
                    part = jnp.dot(
                        window, w[dt, dy].reshape(3 * c2, c2), preferred_element_type=F32
                    )
                    total = part if total is None else total + part
            results.append(total.reshape(frames, out_h, across, c2))
        return results, here + later

    hidden, copies2 = norm_conv(1, raw2, col2, stage2, st2, g2, s2, ca_w, weights[1])
    for b in range(2):
        raw3[2 : 2 + frames, 1 : 1 + out_h, b * across : (b + 1) * across, :] = hidden[b].astype(
            BF16
        )
    branch, copies3 = norm_conv(2, raw3, col3, stage3, st3, g3, s3, cb_w, weights[2])
    for b in range(2):
        lift = raw2[2 : 2 + frames, 1 : 1 + out_h, b * across : (b + 1) * across, :]
        total = lift.astype(F32) + branch[b]
        for k in range(c2 // 128):
            merged[k, :, :, pl.ds(b, across, stride=2), :] = total[..., k * 128 : (k + 1) * 128]
    for k in range(c2 // 128):
        out[:, :, :, k * 128 : (k + 1) * 128] = merged[k].astype(BF16)

    sent(lat_copies)
    sent(copies2)
    sent(copies3)
    for i, st in enumerate((st1, st2, st3)):
        all_stats(st, i, stat_send)


def per_device(sizes, lat, g1, s1, up_w, g2, s2, ca, g3, s3, cb):
    frames, height, across, c1 = lat.shape
    c2 = up_w.shape[-1]
    out_h, out_w = 2 * height, 2 * across
    n_all = sizes[0] * sizes[1] * sizes[2]
    vmem = pl.BlockSpec(memory_space=pltpu.VMEM)
    hbm = pl.BlockSpec(memory_space=pl.ANY)
    field = pltpu.VMEM((frames + 2, out_h + 2, out_w, c2), BF16)
    column = pltpu.VMEM((2, frames + 2, out_h + 2, 1, c2), F32)
    staged = pltpu.VMEM((2, frames, out_h, 1, c2), F32)
    macs = frames * out_h * out_w * 54 * c2 * c2 + frames * height * across * 9 * c1 * c2
    return pl.pallas_call(
        functools.partial(kernel, sizes),
        out_shape=jax.ShapeDtypeStruct((frames, out_h, out_w, c2), BF16),
        in_specs=[vmem, vmem, vmem, hbm, vmem, vmem, hbm, vmem, vmem, hbm],
        out_specs=vmem,
        scratch_shapes=[
            pltpu.VMEM(up_w.shape, BF16),
            pltpu.VMEM(ca.shape, BF16),
            pltpu.VMEM(cb.shape, BF16),
            pltpu.VMEM((frames, across, c1), BF16),
            pltpu.VMEM((frames, height + 1, 1, c1), F32),
            pltpu.VMEM((frames, height, 1, c1), F32),
            pltpu.VMEM((frames, height + 1, across, 2 * c1), BF16),
            field,
            field,
            column,
            column,
            staged,
            staged,
            pltpu.VMEM((frames + 2, out_h + 2, across, 4 * c2), BF16),
            pltpu.VMEM((c2 // 128, frames, out_h, out_w, 128), F32),
            pltpu.VMEM((n_all, 2, c1), F32),
            pltpu.VMEM((n_all, 2, c2), F32),
            pltpu.VMEM((n_all, 2, c2), F32),
            pltpu.SemaphoreType.DMA((3,)),
            pltpu.SemaphoreType.DMA((3, 18)),
            pltpu.SemaphoreType.DMA((3, 18)),
            pltpu.SemaphoreType.DMA((3,)),
            pltpu.SemaphoreType.DMA((3,)),
        ],
        compiler_params=pltpu.CompilerParams(
            collective_id=0, has_side_effects=True, vmem_limit_bytes=44 * 2**20
        ),
        cost_estimate=pl.CostEstimate(
            flops=2 * macs, bytes_accessed=10_000_000, transcendentals=2_000_000
        ),
    )(lat, g1[None], s1[None], up_w, g2[None], s2[None], ca, g3[None], s3[None], cb)


def solution(mesh):
    sizes = (mesh.shape["ha"], mesh.shape["wa"], mesh.shape["ta"])
    fields = P(("videos", "ta"), "ha", "wa", None)
    return jax.shard_map(
        functools.partial(per_device, sizes),
        mesh=mesh,
        in_specs=(fields,) + (P(),) * 9,
        out_specs=fields,
        check_vma=False,
    )
```

time: 205 us -> 44.2 us (0.22)
  blocking collectives: 95.1 us -> 0 us
  Pallas kernels: 0 us -> 32.4 us
  waiting for transfers between devices: 28 us -> 0 us
  matrix products: 24.9 us -> 0 us
  starting transfers between devices: 23.2 us -> 0 us
  other arithmetic: 18.4 us -> 0 us
    psum x3 -> x0, blocking collectives: 95.1 us -> none  [activate(): lax.psum((jnp.sum(grouped, axis=(0, 2)), jnp.sum(grouped * grouped, axis=...]
    pallas_call x0 -> x1, Pallas kernels: none -> 32.4 us  [per_device(): pl.pallas_call(functools.partial(kernel, sizes), out_shape=jax.ShapeDtype...]
    ppermute x12 -> x0, waiting for transfers between devices: 28 us -> none  [the longest x4 13.7 us: padded_2(): after = lax.ppermute(initial, axis, down)]
    ppermute x12 -> x0, starting transfers between devices: 23.2 us -> none  [the longest x4 11.7 us: padded_2(): before = lax.ppermute(last, axis, up)]
    dot_general x60 -> x0, matrix products: 21.3 us -> none  [the longest x54 14.4 us: valid_conv(): jnp.dot(window.reshape(-1, window.shape[-1]), kernel[step_t, step_y, step...]
    concatenate x8 -> x0, other arithmetic: 11.8 us -> none  [the longest x6 10.1 us: padded_2(): x = jnp.concatenate([before, x, after], axis=dim)]
    unnamed x13 -> x21, local copies, waits for them, and re-layouts: 0.35 us -> 11.4 us
    slice x61 -> x0, local copies, waits for them, and re-layouts: 8.4 us -> none  [the longest x56 8.07 us: valid_conv(): padded[step_t:step_t + frames, step_y:step_y + height, step_x:step_x + ac...]
  transfers between devices with their start and end apart: 12 -> 0, of which waited for: 10 -> 0; matrix products, arithmetic and copies ran while one was open for 4% -> 0% of each run, Pallas kernels for 0% -> 0%
where the time goes in v1:
time: 44.2 us; the launch traced here: 43.8 us
  Pallas kernels  32.4 us (73%)
  local copies, waits for them, and re-layouts  11.4 us (26%)
    pallas_call x1, Pallas kernels, per_device(): pl.pallas_call(functools.partial(kernel, sizes), out_shape=jax.ShapeDtype...  32.4 us
    unnamed x21, local copies, waits for them, and re-layouts  11.4 us

profile of v1, /device:TPU:0, one launch (start us, length us, event | category | flops | bytes accessed | tf_op | source)
XLA Modules:
  0.0 43.8 jit_solution(409147458793284456)
XLA Ops:
  0.0 0.0 copy-start
  0.0 2.0 %copy-done = bf16[3,3,3,256,256]{4,3,2,1,0:T(8,128)(2,1)S(1)} copy-done((bf16[3,3,3,256,256]{4,3,2,1,0:T(8,128)(2,1)S(1)}, bf16[3,3,3,256,256]{4,3,2,1,0:T(8,128)(2,1)}, u32[]{:S(2)}) %copy-start) | copy-done | bytes 3538968
  2.0 0.0 copy-start.1
  2.0 2.0 %copy-done.1 = bf16[3,3,3,256,256]{4,3,2,1,0:T(8,128)(2,1)S(1)} copy-done((bf16[3,3,3,256,256]{4,3,2,1,0:T(8,128)(2,1)S(1)}, bf16[3,3,3,256,256]{4,3,2,1,0:T(8,128)(2,1)}, u32[]{:S(2)}) %copy-start.1) | copy-done | bytes 3538968
  4.0 0.0 copy-start.2
  4.0 1.7 %copy-done.2 = bf16[3,3,512,256]{3,2,1,0:T(8,128)(2,1)S(1)} copy-done((bf16[3,3,512,256]{3,2,1,0:T(8,128)(2,1)S(1)}, bf16[3,3,512,256]{3,2,1,0:T(8,128)(2,1)}, u32[]{:S(2)}) %copy-start.2) | copy-done | bytes 2359320
  5.7 0.0 copy-start.3
  5.7 0.9 %copy-done.3 = bf16[3,2,32,512]{3,2,1,0:T(8,128)(2,1)S(1)} copy-done((bf16[3,2,32,512]{3,2,1,0:T(8,128)(2,1)S(1)}, bf16[3,2,32,512]{3,2,1,0:T(8,128)(2,1)}, u32[]{:S(2)}) %copy-start.3) | copy-done | bytes 196632
  6.6 0.0 copy-start.4
  6.6 0.7 %copy-done.4 = f32[512]{0:T(512)S(1)} copy-done((f32[512]{0:T(512)S(1)}, f32[512]{0:T(512)}, u32[]{:S(2)}) %copy-start.4) | copy-done | bytes 2072
  7.3 0.0 copy-start.5
  7.3 0.7 %copy-done.5 = f32[512]{0:T(512)S(1)} copy-done((f32[512]{0:T(512)S(1)}, f32[512]{0:T(512)}, u32[]{:S(2)}) %copy-start.5) | copy-done | bytes 2072
  8.0 0.0 copy-start.6
  8.0 0.7 %copy-done.6 = f32[256]{0:T(256)S(1)} copy-done((f32[256]{0:T(256)S(1)}, f32[256]{0:T(256)}, u32[]{:S(2)}) %copy-start.6) | copy-done | bytes 1048
  8.6 0.0 copy-start.7
  8.6 0.7 %copy-done.7 = f32[256]{0:T(256)S(1)} copy-done((f32[256]{0:T(256)S(1)}, f32[256]{0:T(256)}, u32[]{:S(2)}) %copy-start.7) | copy-done | bytes 1048
  9.3 0.0 copy-start.8
  9.3 0.7 %copy-done.8 = f32[256]{0:T(256)S(1)} copy-done((f32[256]{0:T(256)S(1)}, f32[256]{0:T(256)}, u32[]{:S(2)}) %copy-start.8) | copy-done | bytes 1048
  10.0 0.0 copy-start.9
  10.0 0.7 %copy-done.9 = f32[256]{0:T(256)S(1)} copy-done((f32[256]{0:T(256)S(1)}, f32[256]{0:T(256)}, u32[]{:S(2)}) %copy-start.9) | copy-done | bytes 1048
  10.7 32.4 %shard_map.100 = bf16[3,4,64,256]{3,2,1,0:T(8,128)(2,1)S(1)} custom-call(bf16[3,2,32,512]{3,2,1,0:T(8,128)(2,1)S(1)} %copy-done.3, f32[1,512]{1,0:T(1,128)S(1)} %bitcast.6, f32[1,512]{1,0:T(1,128)S(1)} %bitcast.7, bf16[3,3,512,256]{3,2,1,0:T(8,128)(2,1)S(1)} %copy-done.2, f32[1,256]{1,0:T(1,128)S(1)} %bitcast.8, f32[1,256]{1,0:T(1,128)S(1)} %bitcast.9, ...), custom_call_target="tpu_custom_call" | custom-call | flops 5888802816 | bytes 10000000 | tf_op jit(solution)/shard_map/pallas_call | solution.py:369
  43.1 0.7 %copy.12 = bf16[3,4,64,256]{3,2,1,0:T(8,128)(2,1)} copy(bf16[3,4,64,256]{3,2,1,0:T(8,128)(2,1)S(1)} %shard_map.100) | data formatting | bytes 786432
Async XLA Ops:
  0.0 2.0 %copy-start = (bf16[3,3,3,256,256]{4,3,2,1,0:T(8,128)(2,1)S(1)}, bf16[3,3,3,256,256]{4,3,2,1,0:T(8,128)(2,1)}, u32[]{:S(2)}) copy-start(bf16[3,3,3,256,256]{4,3,2,1,0:T(8,128)(2,1)} %ca_hbm.1) | copy-start | bytes 10616836
  2.0 2.0 %copy-start.1 = (bf16[3,3,3,256,256]{4,3,2,1,0:T(8,128)(2,1)S(1)}, bf16[3,3,3,256,256]{4,3,2,1,0:T(8,128)(2,1)}, u32[]{:S(2)}) copy-start(bf16[3,3,3,256,256]{4,3,2,1,0:T(8,128)(2,1)} %cb_hbm.1) | copy-start | bytes 10616836
  4.0 1.7 %copy-start.2 = (bf16[3,3,512,256]{3,2,1,0:T(8,128)(2,1)S(1)}, bf16[3,3,512,256]{3,2,1,0:T(8,128)(2,1)}, u32[]{:S(2)}) copy-start(bf16[3,3,512,256]{3,2,1,0:T(8,128)(2,1)} %up_hbm.1) | copy-start | bytes 7077892
  5.7 0.9 %copy-start.3 = (bf16[3,2,32,512]{3,2,1,0:T(8,128)(2,1)S(1)}, bf16[3,2,32,512]{3,2,1,0:T(8,128)(2,1)}, u32[]{:S(2)}) copy-start(bf16[3,2,32,512]{3,2,1,0:T(8,128)(2,1)} %lat.1) | copy-start | bytes 589828
  6.6 0.7 %copy-start.4 = (f32[512]{0:T(512)S(1)}, f32[512]{0:T(512)}, u32[]{:S(2)}) copy-start(f32[512]{0:T(512)} %param.11) | copy-start | bytes 6148
  7.3 0.7 %copy-start.5 = (f32[512]{0:T(512)S(1)}, f32[512]{0:T(512)}, u32[]{:S(2)}) copy-start(f32[512]{0:T(512)} %param.12) | copy-start | bytes 6148
  8.0 0.7 %copy-start.6 = (f32[256]{0:T(256)S(1)}, f32[256]{0:T(256)}, u32[]{:S(2)}) copy-start(f32[256]{0:T(256)} %param.14) | copy-start | bytes 3076
  8.6 0.7 %copy-start.7 = (f32[256]{0:T(256)S(1)}, f32[256]{0:T(256)}, u32[]{:S(2)}) copy-start(f32[256]{0:T(256)} %param.15) | copy-start | bytes 3076
  9.3 0.7 %copy-start.8 = (f32[256]{0:T(256)S(1)}, f32[256]{0:T(256)}, u32[]{:S(2)}) copy-start(f32[256]{0:T(256)} %param.17) | copy-start | bytes 3076
  10.0 0.7 %copy-start.9 = (f32[256]{0:T(256)S(1)}, f32[256]{0:T(256)}, u32[]{:S(2)}) copy-start(f32[256]{0:T(256)} %param.18) | copy-start | bytes 3076
